TPU v7x, 512 devices: a whole 4x8x8 slice. The times are simulated.
512 devices in a mesh: replica: 16 (over y, core), fsdp: 32 (over x, z).
Axes of the slice: x: 4, y: 8, z: 8, core: 2. Of those that a mesh axis runs over, the one named last changes fastest.
Arguments:
- momentum: float32 [16, 256, 14336], P('replica', 'fsdp'), may hold values from -6 to 6
- gradient: bfloat16 [16, 256, 14336], P('replica', 'fsdp'), may hold values from -6 to 6
- selection: int32 [16, 4, 224, 2], replicated, may hold values from 0 to 63, as said below
Outputs:
- residual_momentum: float32 [16, 256, 14336], P('replica', 'fsdp')
- update: float32 [256, 14336], P(None, 'fsdp')
Inputs may be any that keep to these rules, and one draw needn't show every extreme that they name: `selection`: for each replica and span, the 2 block numbers are distinct.
All inputs are finite; a program needn't handle non-finite values.
Results may differ from a plain program's by a relative error of at most 0.0003.
Values sent between devices are 32-bit elements; how exact they have to be, the bound alone decides.
A program may use at most 64 MiB of HBM per device.

v0:
```python
import jax
import jax.numpy as jnp
from jax import lax
from jax.sharding import PartitionSpec as P

SPAN_SIDE = 64
BLOCK_SIDE = 8
BLOCKS_KEPT = 2


decay_rate = 0.9
highest = lax.Precision.HIGHEST


def from_everyone(value, axis):
    size = lax.axis_size(axis)
    return lax.all_to_all(
        jnp.broadcast_to(value[None], (size, *value.shape)), axis, 0, 0, tiled=True
    )


def joined_along(tiles, dim):
    shape = list(tiles.shape[1:])
    shape[dim] *= tiles.shape[0]
    return jnp.moveaxis(tiles, 0, dim).reshape(shape)


def gathered_copies(value, axis, dim):
    tiles = from_everyone(value, axis)
    return joined_along(tiles, dim)


def cosine_table(side):
    freq = jnp.arange(side, dtype=jnp.float32)[:, None]
    place = jnp.arange(side, dtype=jnp.float32)[None, :]
    scale = jnp.where(freq == 0, jnp.sqrt(1.0 / side), jnp.sqrt(2.0 / side))
    return scale * jnp.cos(jnp.pi * (2.0 * place + 1.0) * freq / (2.0 * side))


def side_marks(index):
    per_side = SPAN_SIDE // BLOCK_SIDE
    return (index[..., None] == jnp.arange(per_side, dtype=jnp.int32)).astype(jnp.float32)


def pick_rows(index, tiles):
    return jnp.einsum("...p,pia->...ia", side_marks(index), tiles, precision=highest)


def local(momentum, gradient, selection):
    table = cosine_table(SPAN_SIDE)
    per_side = SPAN_SIDE // BLOCK_SIDE
    tiles = table.reshape(per_side, BLOCK_SIDE, SPAN_SIDE)
    zero = jnp.zeros((), jnp.int32)
    fsdp_count = lax.axis_size("fsdp")
    fsdp_rank = lax.axis_index("fsdp")
    replica_rank = lax.axis_index("replica")
    replicas = selection.shape[0]
    decayed = decay_rate * momentum[0] + gradient[0].astype(jnp.float32)
    rows_dev, width = decayed.shape
    rows_all = rows_dev * fsdp_count
    span_rows = rows_all // SPAN_SIDE
    local_cols = width // fsdp_count
    span_cols = local_cols // SPAN_SIDE
    all_cols = width // SPAN_SIDE
    group = SPAN_SIDE // rows_dev
    span_row_own = fsdp_rank // group
    square = BLOCK_SIDE * BLOCK_SIDE
    column_start = fsdp_rank * span_cols
    chosen_all = lax.dynamic_slice(
        selection, (zero, zero, column_start, zero), (replicas, span_rows, span_cols, BLOCKS_KEPT)
    )
    chosen_own = lax.dynamic_index_in_dim(chosen_all, replica_rank, 0, keepdims=False)
    row_own = pick_rows(chosen_own // per_side, tiles)
    col_own = pick_rows(chosen_own % per_side, tiles)
    mine_all = lax.dynamic_slice(
        selection, (replica_rank, span_row_own, zero, zero), (1, 1, all_cols, BLOCKS_KEPT)
    )
    mine_all = mine_all.reshape(all_cols, BLOCKS_KEPT)
    owned = lax.all_to_all(decayed, "fsdp", split_axis=1, concat_axis=0, tiled=True)
    spans = owned.reshape(span_rows, SPAN_SIDE, span_cols, SPAN_SIDE)
    kept = jnp.einsum("rckia,racb,rckjb->rckij", row_own, spans, col_own, precision=highest)
    kept = kept.reshape(span_rows, span_cols, BLOCKS_KEPT, square)
    packed = kept.reshape(1, span_rows, span_cols, BLOCKS_KEPT * square)
    piece = gathered_copies(packed, "replica", 0)
    count = piece.shape[0]
    values = piece.reshape(count, span_rows, span_cols, BLOCKS_KEPT, BLOCK_SIDE, BLOCK_SIDE)
    row_sel = pick_rows(chosen_all // per_side, tiles)
    col_sel = pick_rows(chosen_all % per_side, tiles)
    summed = jnp.einsum("qrckia,qrckij,qrckjb->racb", row_sel, values, col_sel, precision=highest)
    update = summed.reshape(rows_all, local_cols)
    own_values = kept.reshape(span_rows, span_cols, BLOCKS_KEPT, BLOCK_SIDE, BLOCK_SIDE)
    extracted = jnp.einsum(
        "rckia,rckij,rckjb->racb", row_own, own_values, col_own, precision=highest
    )
    extracted = extracted.reshape(rows_all, local_cols)
    taken = lax.all_to_all(extracted, "fsdp", split_axis=0, concat_axis=1, tiled=True)
    residual_momentum = decayed - taken
    return (residual_momentum[None], update)


def solution(mesh):
    placed = (P("replica", "fsdp", None), P("replica", "fsdp", None), P())
    return jax.shard_map(
        local,
        mesh=mesh,
        in_specs=placed,
        out_specs=(P("replica", "fsdp", None), P(None, "fsdp")),
        check_vma=False,
    )
```

profile of v0, /device:TPU:1, one launch (start us, length us, event | category | flops | bytes accessed | tf_op | source)
XLA Modules:
  0.0 84.9 jit_solution(9852488467808630540)
XLA Ops:
  0.6 1.2 %convert_add_fusion = f32[1,8,14336]{2,1,0:T(8,128)S(1)} fusion(bf16[1,8,14336]{2,1,0:T(8,128)(2,1)} %param.4, f32[1,8,14336]{2,1,0:T(8,128)} %param.3), kind=kLoop, calls=%fused_computation.9 | loop fusion | flops 344064 | bytes 1146880 | tf_op jit(solution)/shard_map/add | solution.py:58
  1.9 0.3 add.64
  2.1 1.1 %copy.44 = f32[8,32,448]{2,0,1:T(8,128)} copy(f32[8,32,448]{2,1,0:T(8,128)S(1)} %add.64) | data formatting | bytes 917504 | tf_op jit(solution)/shard_map/add | solution.py:58
  3.2 13.7 %all-to-all-start = ((f32[8,32,448]{2,0,1:T(8,128)}), f32[8,32,448]{2,0,1:T(8,128)S(1)}, u32[]{:S(2)}, u32[]{:S(2)}) async-start(f32[8,32,448]{2,0,1:T(8,128)} %copy.44), calls=%async_computation | async-start | bytes 1048576 | tf_op jit(solution)/shard_map/all_to_all | solution.py:79
  17.0 0.3 and_select_fusion.1
  17.6 0.1 copy.61
  17.7 0.4 fusion.30
  18.2 0.4 fusion.28
  18.6 3.6 %fusion.13 = f32[16,4,7,2,8,64]{5,0,4,3,2,1:T(8,128)} fusion(s32[16,4,7,2]{0,3,2,1:T(2,128)S(1)} %copy.58, f32[8,8]{0,1:T(8,128)S(1)} %multiply_add_fusion, f32[64]{0:T(128)S(1)} %add_multiply_fusion, f32[8,8]{0,1:T(8,128)S(1)} %compare_select_fusion), kind=kOutput, calls=%fused_computation.13 | convolution fusion | flops 44059648 | bytes 1839360 | tf_op jit(solution)/shard_map/...p,pia->...ia/dot_general | solution.py:46
  22.2 9.0 %all-to-all-done = f32[8,32,448]{2,0,1:T(8,128)S(1)} async-done(((f32[8,32,448]{2,0,1:T(8,128)}), f32[8,32,448]{2,0,1:T(8,128)S(1)}, u32[]{:S(2)}, u32[]{:S(2)}) %all-to-all-start) | async-done | bytes 458784 | tf_op jit(solution)/shard_map/all_to_all | solution.py:79
  31.3 0.2 reshape.116
  31.5 1.0 %fusion.10 = f32[4,7,64,2,8]{2,4,3,1,0:T(8,128)S(1)} fusion(f32[4,64,7,64,1]{3,2,1,0,4:T(8,128)S(1)} %bitcast.78, f32[4,7,2,8,64]{4,1,3,2,0:T(8,128)S(1)} %fusion.30), kind=kOutput, calls=%fused_computation.7 | convolution fusion | flops 22020096 | bytes 688128 | tf_op jit(solution)/shard_map/rckia,racb,rckjb->rckij/dot_general | solution.py:81
  32.5 0.5 fusion.19
  33.0 0.1 reshape.127
  33.2 0.7 broadcast_in_dim.15
  33.9 10.6 %all-to-all-start.2 = ((f32[16,1,4,7,128]{4,2,3,1,0:T(4,128)}), f32[16,1,4,7,128]{4,2,3,1,0:T(4,128)S(1)}, u32[]{:S(2)}, u32[]{:S(2)}) async-start(f32[16,1,4,7,128]{4,2,3,1,0:T(4,128)} %broadcast_in_dim.15), calls=%async_computation.2 | async-start | bytes 458752 | tf_op jit(solution)/shard_map/all_to_all | solution.py:17
  44.5 3.6 %fusion.16 = f32[16,4,7,2,8,64]{5,0,4,3,2,1:T(8,128)} fusion(s32[16,4,7,2]{0,3,2,1:T(2,128)S(1)} %copy.61, f32[8,8]{0,1:T(8,128)S(1)} %multiply_add_fusion, f32[64]{0:T(128)S(1)} %add_multiply_fusion, f32[8,8]{0,1:T(8,128)S(1)} %compare_select_fusion), kind=kOutput, calls=%fused_computation.15 | convolution fusion | flops 44059648 | bytes 1839360 | tf_op jit(solution)/shard_map/...p,pia->...ia/dot_general | solution.py:46
  48.1 0.6 fusion.21
  48.7 1.6 %convolution_bitcast_fusion = f32[4,64,7,64]{3,1,2,0:T(8,128)S(1)} fusion(f32[4,7,2,8,64]{4,3,2,1,0:T(8,128)S(1)} %fusion.21, f32[4,7,2,8,64]{4,1,3,2,0:T(8,128)S(1)} %fusion.28), kind=kOutput, calls=%fused_computation.5 | convolution fusion | flops 22020096 | bytes 688128 | tf_op jit(solution)/shard_map/rckia,rckij,rckjb->racb/dot_general | solution.py:92
  50.4 0.5 copy.54
  50.9 1.0 %all_to_all.29 = f32[32,8,448]{2,1,0:T(8,128)} reshape(f32[4,64,7,64]{3,2,1,0:T(8,128)S(1)} %copy.54) | data formatting | bytes 917504 | tf_op jit(solution)/shard_map/all_to_all | solution.py:96
  51.9 3.7 %all-to-all-done.2 = f32[16,1,4,7,128]{4,2,3,1,0:T(4,128)S(1)} async-done(((f32[16,1,4,7,128]{4,2,3,1,0:T(4,128)}), f32[16,1,4,7,128]{4,2,3,1,0:T(4,128)S(1)}, u32[]{:S(2)}, u32[]{:S(2)}) %all-to-all-start.2) | async-done | bytes 229408 | tf_op jit(solution)/shard_map/all_to_all | solution.py:17
  55.6 5.5 %all-to-all-start.1 = ((f32[32,8,448]{2,1,0:T(8,128)}), f32[32,8,448]{2,1,0:T(8,128)S(1)}, u32[]{:S(2)}, u32[]{:S(2)}) async-start(f32[32,8,448]{2,1,0:T(8,128)} %all_to_all.29), calls=%async_computation.1 | async-start | bytes 1048576 | tf_op jit(solution)/shard_map/all_to_all | solution.py:96
  61.1 0.5 copy.57
  61.7 4.1 %copy.73 = f32[16,4,7,2,8,8]{4,5,3,1,2,0:T(8,128)} copy(f32[16,4,7,2,8,8]{0,5,4,3,2,1:T(8,128)S(1)} %bitcast.77) | data formatting | bytes 458752 | tf_op jit(solution)/shard_map/reshape;reshape | solution.py:86
  65.7 9.2 %fusion.2 = f32[16,4,7,2,8,64]{5,4,3,1,2,0:T(8,128)S(1)} fusion(f32[16,4,7,2,8,8]{4,5,3,1,2,0:T(8,128)} %copy.73, f32[16,4,7,2,8,64]{5,0,4,3,2,1:T(8,128)} %fusion.13), kind=kOutput, calls=%fused_computation.2 | convolution fusion | flops 44040192 | bytes 3899392 | tf_op jit(solution)/shard_map/qrckia,qrckij,qrckjb->racb/dot_general | solution.py:89
  75.0 6.9 %fusion.5 = f32[4,64,7,64]{3,1,2,0:T(8,128)S(1)} fusion(f32[16,4,7,2,8,64]{5,0,4,3,2,1:T(8,128)S(1)} %copy-done, f32[16,4,7,2,8,64]{5,4,3,1,2,0:T(8,128)S(1)} %fusion.2), kind=kOutput, calls=%fused_computation.6 | convolution fusion | flops 352321536 | bytes 4128768 | tf_op jit(solution)/shard_map/qrckia,qrckij,qrckjb->racb/dot_general | solution.py:89
  81.9 0.4 copy.64
  82.2 1.3 %reshape.117 = f32[256,448]{0,1:T(8,128)} reshape(f32[4,64,7,64]{1,0,3,2:T(4,128)S(1)} %copy.64) | data formatting | bytes 917504 | tf_op jit(solution)/shard_map/reshape | solution.py:90
  83.6 0.3 copy.55
  83.9 0.2 all_to_all.32
  84.1 0.8 sub.17
  (14 shorter events, 0.3 us)
Async XLA Ops:
  0.6 16.4 %copy-start.1 = (s32[16,4,224,2]{2,3,1,0:T(2,128)S(1)}, s32[16,4,224,2]{2,3,1,0:T(2,128)}, u32[]{:S(2)}) copy-start(s32[16,4,224,2]{2,3,1,0:T(2,128)} %param.5) | copy-start | bytes 344068
  3.2 28.0 %all-to-all-start = ((f32[8,32,448]{2,0,1:T(8,128)}), f32[8,32,448]{2,0,1:T(8,128)S(1)}, u32[]{:S(2)}, u32[]{:S(2)}) async-start(f32[8,32,448]{2,0,1:T(8,128)} %copy.44), calls=%async_computation | async-start | bytes 1048576 | tf_op jit(solution)/shard_map/all_to_all | solution.py:79
  33.9 21.7 %all-to-all-start.2 = ((f32[16,1,4,7,128]{4,2,3,1,0:T(4,128)}), f32[16,1,4,7,128]{4,2,3,1,0:T(4,128)S(1)}, u32[]{:S(2)}, u32[]{:S(2)}) async-start(f32[16,1,4,7,128]{4,2,3,1,0:T(4,128)} %broadcast_in_dim.15), calls=%async_computation.2 | async-start | bytes 458752 | tf_op jit(solution)/shard_map/all_to_all | solution.py:17
  55.6 28.0 %all-to-all-start.1 = ((f32[32,8,448]{2,1,0:T(8,128)}), f32[32,8,448]{2,1,0:T(8,128)S(1)}, u32[]{:S(2)}, u32[]{:S(2)}) async-start(f32[32,8,448]{2,1,0:T(8,128)} %all_to_all.29), calls=%async_computation.1 | async-start | bytes 1048576 | tf_op jit(solution)/shard_map/all_to_all | solution.py:96
  65.7 9.2 %copy-start = (f32[16,4,7,2,8,64]{5,0,4,3,2,1:T(8,128)S(1)}, f32[16,4,7,2,8,64]{5,0,4,3,2,1:T(8,128)}, u32[]{:S(2)}) copy-start(f32[16,4,7,2,8,64]{5,0,4,3,2,1:T(8,128)} %fusion.16) | copy-start | bytes 5505028
where the time goes:
time: 85.4 us; the launch traced here: 84.9 us
  starting transfers between devices  29.9 us (35%)
  matrix products  27.9 us (33%)
  waiting for transfers between devices  12.7 us (15%)
  local copies, waits for them, and re-layouts  11.2 us (13%)
  other arithmetic  2.38 us (3%)
    dot_general x2, matrix products, local(): jnp.einsum('qrckia,qrckij,qrckjb->racb', row_sel, values, col_sel, precis...  16.1 us
    all_to_all x1, starting transfers between devices, local(): lax.all_to_all(decayed, 'fsdp', split_axis=1, concat_axis=0, tiled=True)  13.7 us
    all_to_all x1, starting transfers between devices, from_everyone(): lax.all_to_all(jnp.broadcast_to(value[None], (size, *value.shape)), axis,...  10.6 us
    all_to_all x1, waiting for transfers between devices, local(): lax.all_to_all(decayed, 'fsdp', split_axis=1, concat_axis=0, tiled=True)  9.05 us
    dot_general x4, matrix products, pick_rows(): jnp.einsum('...p,pia->...ia', side_marks(index), tiles, precision=highest)  8.08 us
    all_to_all x1, starting transfers between devices, local(): lax.all_to_all(extracted, 'fsdp', split_axis=0, concat_axis=1, tiled=True)  5.52 us
    another operation x1, local copies, waits for them, and re-layouts, local(): piece.reshape(count, span_rows, span_cols, BLOCKS_KEPT, BLOCK_SIDE, BLOCK...  4.08 us
    all_to_all x1, waiting for transfers between devices, from_everyone(): lax.all_to_all(jnp.broadcast_to(value[None], (size, *value.shape)), axis,...  3.65 us
  transfers between devices with their start and end apart: 3, of which 2 were waited for; matrix products, arithmetic and copies ran while one was open for 40% of the time, Pallas kernels for 0%

commit v1 on v0

v1 whole, which is shorter than its diff:
```python
import functools

import jax
import jax.numpy as jnp
import numpy as np
from jax import lax
from jax.experimental import pallas as pl
from jax.experimental.pallas import tpu as pltpu
from jax.sharding import PartitionSpec as P

SIDE = 64
BLOCK = 8
MESH = pl.DeviceIdType.MESH
F32 = jnp.float32
BF16 = jnp.bfloat16


def cosine_table():
    freq = np.arange(SIDE, dtype=np.float64)[:, None]
    place = np.arange(SIDE, dtype=np.float64)[None, :]
    scale = np.where(freq == 0, np.sqrt(1.0 / SIDE), np.sqrt(2.0 / SIDE))
    return scale * np.cos(np.pi * (2.0 * place + 1.0) * freq / (2.0 * SIDE))


def halves_np(value):
    value = value.astype(np.float32)
    high = value.astype(BF16)
    low = (value - high.astype(np.float32)).astype(BF16)
    return high, low


def tables(spans, devices_z):
    table = cosine_table()
    spread = np.zeros((8 * SIDE, 8, 8, BLOCK))
    for s in range(spans):
        spread[s * SIDE:(s + 1) * SIDE, :, s, :] = table.T.reshape(SIDE, 8, BLOCK)
    spread = np.stack(halves_np(spread.reshape(8 * SIDE, 8 * SIDE)))
    cube = table.reshape(8, BLOCK, devices_z, 8)
    by_a = cube.transpose(2, 3, 1, 0).reshape(devices_z, 64, 8)
    by_u = cube.transpose(2, 1, 3, 0).reshape(devices_z, 64, 8)
    rows = np.concatenate([by_a, by_u], axis=1)
    rows = np.concatenate(halves_np(rows), axis=-1)
    high, low = halves_np(table.T)
    inverse = np.concatenate([high, high, low], axis=1)
    return spread, rows, inverse


def halves(value):
    high = value.astype(BF16)
    low = (value - high.astype(F32)).astype(BF16)
    return high, low


def dot(a, b):
    return jnp.dot(a, b, preferred_element_type=F32)


def dot_t(a, b):
    return lax.dot_general(a, b, (((1,), (1,)), ((), ())), preferred_element_type=F32)


def kernel(
    nx, nz, nq, spans,
    mom_hbm, grad_hbm, sel_ref, spread_hbm, rows_hbm, inv_ref,
    res_ref, upd_ref,
    mom, grad, spread, rows, decayed, lhs, blk, blk_q, weights, part, arrived, kept, full, gathered, upd_half, res_buf,
    load_sem, send_sem, part_sem, full_sem, gather_sem, upd_send, upd_recv, out_sem,
):
    replica = lax.axis_index("replica")
    fsdp = lax.axis_index("fsdp")
    x, z = fsdp // nz, lax.rem(fsdp, nz)
    core = lax.rem(replica, 2)
    sibling = replica + 1 - 2 * core
    per_core = nx // 2
    width = spans * SIDE
    owners = nx * nz

    barrier = pltpu.get_barrier_semaphore()

    load_mom = pltpu.make_async_copy(mom_hbm, mom, load_sem.at[0])
    load_grad = pltpu.make_async_copy(grad_hbm, grad, load_sem.at[1])
    load_rows = pltpu.make_async_copy(rows_hbm.at[z], rows, load_sem.at[2])
    load_spread = pltpu.make_async_copy(spread_hbm, spread, load_sem.at[3])
    load_rows.start()
    load_mom.start()
    load_grad.start()
    load_spread.start()

    def greet_z(d, _):
        peer = x * nz + lax.rem(z + d, nz)
        pl.semaphore_signal(barrier, inc=1, device_id=(replica, peer), device_id_type=MESH)
        return 0

    lax.fori_loop(1, nz, greet_z, 0)

    def greet_plane(d, _):
        q = lax.rem(d, nq)
        xs = per_core * core + d // nq

        @pl.when(jnp.logical_or(q != replica, xs != x))
        def _():
            pl.semaphore_signal(barrier, inc=1, device_id=(q, xs * nz + z), device_id_type=MESH)

        return 0

    lax.fori_loop(0, per_core * nq, greet_plane, 0)
    pl.semaphore_signal(barrier, inc=1, device_id=(sibling, fsdp), device_id_type=MESH)

    lane = lax.broadcasted_iota(jnp.int32, (8, 128), 1)
    half = lane // 64
    sub16 = lax.broadcasted_iota(jnp.int32, (16, 128), 0) & 7

    all_cols = owners * spans
    at_own = (replica * nx + x) * 2
    col = lax.broadcasted_iota(jnp.int32, (owners, all_cols), 1)
    row = lax.broadcasted_iota(jnp.int32, (owners, all_cols), 0) * spans
    inside = jnp.logical_and(col >= row, col < row + spans)
    c_f = lax.broadcasted_iota(jnp.int32, (all_cols, 128), 0).astype(F32)
    c_mod = c_f - spans * jnp.floor((c_f + 0.5) * (1.0 / spans))
    l_i = lax.broadcasted_iota(jnp.int32, (all_cols, 128), 1)
    l_s = ((l_i & 63) // 8).astype(F32)
    placed = None
    for k in range(2):
        left = jnp.where(inside, jnp.broadcast_to(sel_ref[pl.ds(at_own + k, 1), :], (owners, all_cols)), 0).astype(F32)
        right = jnp.where(jnp.logical_and(c_mod == l_s, l_i // 64 == k), 1.0, 0.0)
        term = dot(left.astype(BF16), right.astype(BF16))
        placed = term if placed is None else placed + term
    blk[...] = placed.astype(jnp.int32)

    load_rows.wait()
    for f in range(0, owners, 2):
        ones = []
        for g in (f, f + 1):
            i_sel = jnp.broadcast_to(blk[g:g + 1, :], (16, 128)) // 8
            ones.append(jnp.where(i_sel == sub16, 1.0, 0.0).astype(BF16))
        weights[:, f * 128:(f + 2) * 128] = dot(rows[...], jnp.concatenate(ones, axis=1))

    load_mom.wait()
    load_grad.wait()
    decayed[...] = 0.9 * mom[...] + grad[...].astype(F32)

    for p in range(owners // 2):
        base = 2 * width * p
        even = decayed[:, base:base + 8 * SIDE]
        odd = pltpu.roll(decayed[:, base + width - 64:base + 2 * width], 8 * SIDE - 64, 1)
        high, low = halves(jnp.concatenate([even, odd], axis=0))
        lhs[0, 16 * p:16 * p + 16, :] = high
        lhs[1, 16 * p:16 * p + 16, :] = low

    load_spread.wait()

    def selected(f):
        both = jnp.broadcast_to(blk[f:f + 1, :], (8, 128)) & 7
        return both, pltpu.roll(both, 64, 1)

    group = 64
    for m in range(owners * 8 // group):
        at = slice(m * group, (m + 1) * group)
        coeff = dot(lhs[0, at, :], spread[0]) + dot(lhs[1, at, :], spread[0]) + dot(lhs[0, at, :], spread[1])
        for g in range(group // 8):
            f = m * (group // 8) + g
            j_own, j_other = selected(f)
            direct = other = jnp.zeros((8, 128), F32)
            for t in range(4):
                piece = coeff[8 * g:8 * g + 8, 128 * t:128 * t + 128]
                direct = jnp.where(j_own // 2 == t, piece, direct)
                other = jnp.where(j_other // 2 == t, piece, other)
            picked = jnp.where((j_own & 1) == half, direct, pltpu.roll(other, 64, 1))
            total = None
            for a in range(8):
                term = weights[8 * a:8 * a + 8, f * 128:f * 128 + 128] * jnp.broadcast_to(picked[a:a + 1, :], (8, 128))
                total = term if total is None else total + term
            part[f % nz, f // nz] = total

    pl.semaphore_wait(barrier, nz - 1 + per_core * 0 + nx * (nq // 2) - jnp.where(core == x // per_core, 1, 0) + 1)

    def send_part(d, _):
        zt = lax.rem(z + d, nz)
        pltpu.make_async_remote_copy(
            part.at[zt], arrived.at[z], send_sem.at[0], part_sem,
            device_id=(replica, x * nz + zt), device_id_type=MESH,
        ).start()
        return 0

    lax.fori_loop(1, nz, send_part, 0)
    local = pltpu.make_async_copy(part.at[z], arrived.at[z], part_sem)
    local.start()

    c_own = lax.broadcasted_iota(jnp.int32, (all_cols, 128), 0) - spans * fsdp
    s_own = (lax.broadcasted_iota(jnp.int32, (all_cols, 128), 1) & 63) // 8
    pick = jnp.where(jnp.logical_and(c_own == s_own, s_own < spans), 1.0, 0.0).astype(BF16)
    blk_q[...] = dot(sel_ref[...].astype(F32).astype(BF16), pick).astype(jnp.int32)

    pltpu.make_async_copy(arrived, arrived, part_sem).wait()
    for xt in range(nx):
        total = arrived[0, xt]
        for zs in range(1, nz):
            total = total + arrived[zs, xt]
        kept[xt] = total

    def send_plane(d, _):
        xt = d // (nq // 2)
        qt = 2 * lax.rem(d, nq // 2) + x // per_core

        slot = gathered.at[lax.rem(x, per_core) * nq + replica]

        @pl.when(jnp.logical_or(qt != replica, xt != x))
        def _():
            pltpu.make_async_remote_copy(
                kept.at[xt], slot, send_sem.at[1], gather_sem,
                device_id=(qt, xt * nz + z), device_id_type=MESH,
            ).start()

        @pl.when(jnp.logical_and(qt == replica, xt == x))
        def _():
            pltpu.make_async_copy(kept.at[xt], slot, gather_sem).start()

        return 0

    def send_full(d, _):
        zt = lax.rem(z + d, nz)
        pltpu.make_async_remote_copy(
            kept, full.at[z], send_sem.at[2], full_sem,
            device_id=(replica, x * nz + zt), device_id_type=MESH,
        ).start()
        return 0

    lax.fori_loop(1, nz, send_full, 0)
    lax.fori_loop(0, nx * (nq // 2), send_plane, 0)
    pltpu.make_async_copy(kept, full.at[z], full_sem).start()

    pltpu.make_async_copy(full, full, full_sem).wait()
    for p in range(owners // 2):
        parts = []
        for f in (2 * p, 2 * p + 1):
            j_own, j_other = selected(f)
            block = full[f % nz, f // nz]
            total = None
            for u in range(8):
                term = weights[64 + 8 * u:72 + 8 * u, f * 128:f * 128 + 128] * jnp.broadcast_to(block[u:u + 1, :], (8, 128))
                total = term if total is None else total + term
            other = pltpu.roll(total, 64, 1)
            parts.append(jnp.concatenate([
                jnp.where(j_own == 2 * t + half, total, 0.0) + jnp.where(j_other == 2 * t + half, other, 0.0)
                for t in range(4)
            ], axis=1))
        high, low = halves(jnp.concatenate(parts, axis=0))
        lhs[0, 16 * p:16 * p + 16, :] = high
        lhs[1, 16 * p:16 * p + 16, :] = low
    for m in range(owners * 8 // group):
        at = slice(m * group, (m + 1) * group)
        space = dot_t(lhs[0, at, :], spread[0]) + dot_t(lhs[1, at, :], spread[0]) + dot_t(lhs[0, at, :], spread[1])
        for g in range(0, group // 8, 2):
            f = m * (group // 8) + g
            pair = jnp.concatenate([space[8 * g:8 * g + 8, :width], space[8 * g + 8:8 * g + 16, :width]], axis=1)
            at_cols = slice(f * width, (f + 2) * width)
            res_buf[:, at_cols] = decayed[:, at_cols] - pair
    store_res = pltpu.make_async_copy(res_buf, res_ref, out_sem.at[0])
    store_res.start()

    pltpu.make_async_copy(gathered, gathered, gather_sem).wait()
    spatial = []
    for r in range(per_core):
        strips = []
        for t in range(4):
            def add_replica(q, sums, r=r, t=t):
                value = gathered[r * nq + q]
                at = (q * nx + per_core * core + r) * 2
                numbers = jnp.where(half == 0, jnp.broadcast_to(blk_q[pl.ds(at, 1), :], (8, 128)), jnp.broadcast_to(blk_q[pl.ds(at + 1, 1), :], (8, 128)))
                other_numbers = pltpu.roll(numbers, 64, 1)
                other = pltpu.roll(value, 64, 1)
                j_here = 2 * t + half
                here = jnp.where((numbers & 7) == j_here, value, 0.0)
                there = jnp.where((other_numbers & 7) == j_here, other, 0.0)
                i_here, i_there = numbers // 8, other_numbers // 8
                return tuple(
                    sums[i] + jnp.where(i_here == i, here, 0.0) + jnp.where(i_there == i, there, 0.0)
                    for i in range(8)
                )

            sums = lax.fori_loop(0, nq, add_replica, tuple(jnp.zeros((8, 128), F32) for _ in range(8)))
            strips.append(jnp.concatenate(sums, axis=0))
        high, low = halves(jnp.concatenate(strips, axis=1))
        spatial.append(dot(inv_ref[...], jnp.concatenate([high, low, high], axis=0)))
    high, low = halves(jnp.concatenate(spatial, axis=0))
    g_high, g_low = spread[0, :width, :], spread[1, :width, :]
    upd_half[...] = dot_t(g_high, high) + dot_t(g_high, low) + dot_t(g_low, high)
    lanes = per_core * SIDE
    place = upd_ref.at[:, pl.ds(pl.multiple_of(core * lanes, lanes), lanes)]
    send_upd = pltpu.make_async_remote_copy(
        upd_half, place, upd_send, upd_recv, device_id=(sibling, fsdp), device_id_type=MESH
    )
    send_upd.start()
    store_upd = pltpu.make_async_copy(upd_half, place, out_sem.at[1])
    store_upd.start()

    pltpu.make_async_copy(part.at[pl.ds(0, nz - 1)], part.at[pl.ds(0, nz - 1)], send_sem.at[0]).wait()
    pltpu.make_async_copy(full.at[pl.ds(0, nz - 1)], full.at[pl.ds(0, nz - 1)], send_sem.at[2]).wait()
    sent = gathered.at[pl.ds(1, per_core * nq - 1)]

    @pl.when(core == x // per_core)
    def _():
        pltpu.make_async_copy(sent, sent, send_sem.at[1]).wait()

    @pl.when(core != x // per_core)
    def _():
        pltpu.make_async_copy(gathered, gathered, send_sem.at[1]).wait()

    store_res.wait()
    store_upd.wait()
    send_upd.wait()


def local(nx, nz, nq, momentum, gradient, selection):
    rows_dev, all_width = momentum.shape[1:]
    owners = nx * nz
    width = all_width // owners
    spans = width // SIDE
    spread, rows, inverse = tables(spans, nz)
    sel = selection.transpose(0, 1, 3, 2).reshape(nq * nx * 2, owners * spans)
    per_core = nx // 2
    hbm = pl.BlockSpec(memory_space=pl.ANY)
    vmem = pl.BlockSpec(memory_space=pltpu.VMEM)
    dma = pltpu.SemaphoreType.DMA
    res, upd = pl.pallas_call(
        functools.partial(kernel, nx, nz, nq, spans),
        out_shape=(
            jax.ShapeDtypeStruct((rows_dev, all_width), F32),
            jax.ShapeDtypeStruct((width, nx * SIDE), F32),
        ),
        in_specs=[hbm, hbm, vmem, hbm, hbm, vmem],
        out_specs=(hbm, hbm),
        scratch_shapes=[
            pltpu.VMEM((rows_dev, all_width), F32),
            pltpu.VMEM((rows_dev, all_width), BF16),
            pltpu.VMEM(spread.shape, BF16),
            pltpu.VMEM(rows.shape[1:], BF16),
            pltpu.VMEM((rows_dev, all_width), F32),
            pltpu.VMEM((2, owners * 8, 8 * SIDE), BF16),
            pltpu.VMEM((owners, 128), jnp.int32),
            pltpu.VMEM((nq * nx * 2, 128), jnp.int32),
            pltpu.VMEM((128, owners * 128), F32),
            pltpu.VMEM((nz, nx, 8, 128), F32),
            pltpu.VMEM((nz, nx, 8, 128), F32),
            pltpu.VMEM((nx, 8, 128), F32),
            pltpu.VMEM((nz, nx, 8, 128), F32),
            pltpu.VMEM((per_core * nq, 8, 128), F32),
            pltpu.VMEM((width, per_core * SIDE), F32),
            pltpu.VMEM((rows_dev, all_width), F32),
            dma((4,)), dma((3,)), dma, dma, dma, dma, dma, dma((2,)),
        ],
        compiler_params=pltpu.CompilerParams(
            collective_id=0, has_side_effects=True, vmem_limit_bytes=24 * 1024 * 1024
        ),
    )(momentum[0], gradient[0], sel, jnp.asarray(spread), jnp.asarray(rows), jnp.asarray(inverse))
    return res[None], upd.T


def solution(mesh):
    nq = mesh.shape["replica"]
    nz = 8
    nx = mesh.shape["fsdp"] // nz
    return jax.shard_map(
        functools.partial(local, nx, nz, nq),
        mesh=mesh,
        in_specs=(P("replica", "fsdp", None), P("replica", "fsdp", None), P()),
        out_specs=(P("replica", "fsdp", None), P(None, "fsdp")),
        check_vma=False,
    )
```

time: 85.4 us -> 50.9 us (0.60)
  Pallas kernels: 0 us -> 43.4 us
  starting transfers between devices: 29.9 us -> 0 us
  matrix products: 27.9 us -> 0 us
  waiting for transfers between devices: 12.7 us -> 0 us
  local copies, waits for them, and re-layouts: 11.2 us -> 6.51 us
  other arithmetic: 2.38 us -> 0 us
    pallas_call x0 -> x1, Pallas kernels: none -> 43.4 us  [local(): pl.pallas_call(functools.partial(kernel, nx, nz, nq, spans), out_shape=(j...]
    all_to_all x3 -> x0, starting transfers between devices: 29.9 us -> none  [the longest x1 13.7 us: local(): lax.all_to_all(decayed, 'fsdp', split_axis=1, concat_axis=0, tiled=True)]
    dot_general x10 -> x0, matrix products: 27.9 us -> none  [the longest x2 16.1 us: local(): jnp.einsum('qrckia,qrckij,qrckjb->racb', row_sel, values, col_sel, precis...]
    all_to_all x3 -> x0, waiting for transfers between devices: 12.7 us -> none  [the longest x1 9.05 us: local(): lax.all_to_all(decayed, 'fsdp', split_axis=1, concat_axis=0, tiled=True)]
    unnamed x4 -> x12, local copies, waits for them, and re-layouts: 0.01 us -> 5.48 us
    another operation x1 -> x0, local copies, waits for them, and re-layouts: 4.08 us -> none  [local(): piece.reshape(count, span_rows, span_cols, BLOCKS_KEPT, BLOCK_SIDE, BLOCK...]
    all_to_all x4 -> x0, local copies, waits for them, and re-layouts: 2.09 us -> none  [the longest x3 1.55 us: local(): lax.all_to_all(extracted, 'fsdp', split_axis=0, concat_axis=1, tiled=True)]
    add x2 -> x0, local copies, waits for them, and re-layouts: 1.36 us -> none  [local(): decayed = decay_rate * momentum[0] + gradient[0].astype(jnp.float32)]
  transfers between devices with their start and end apart: 3 -> 0, of which waited for: 2 -> 0; matrix products, arithmetic and copies ran while one was open for 40% -> 0% of each run, Pallas kernels for 0% -> 0%
where the time goes in v1:
time: 50.9 us; the launch traced here: 50.6 us
  Pallas kernels  43.4 us (85%)
  local copies, waits for them, and re-layouts  6.51 us (13%)
  between operations  0.67 us (1%)
    pallas_call x1, Pallas kernels, local(): pl.pallas_call(functools.partial(kernel, nx, nz, nq, spans), out_shape=(j...  43.4 us
    unnamed x12, local copies, waits for them, and re-layouts  5.48 us
    reshape x1, local copies, waits for them, and re-layouts, local(): sel = selection.transpose(0, 1, 3, 2).reshape(nq * nx * 2, owners * spans)  1.04 us

profile of v1, /device:TPU:1, one launch (start us, length us, event | category | flops | bytes accessed | tf_op | source)
XLA Modules:
  0.0 50.6 jit_solution(15773186171273758021)
XLA Ops:
  0.6 0.0 copy-start.2
  0.6 1.0 %reshape.7.sel_ref = s32[128,224]{1,0:T(8,128)S(1)} reshape(s32[16,4,2,224]{3,2,1,0:T(2,128)} %bitcast.9) | data formatting | bytes 229376 | tf_op jit(solution)/shard_map/reshape | solution.py:320
  1.7 0.0 copy-done.2
  1.7 0.0 copy-start
  1.7 1.2 %copy-done = bf16[2,512,512]{2,1,0:T(8,128)(2,1)S(1)} copy-done((bf16[2,512,512]{2,1,0:T(8,128)(2,1)S(1)}, bf16[2,512,512]{2,1,0:T(8,128)(2,1)}, u32[]{:S(2)}) %copy-start) | copy-done | bytes 1048600
  2.9 0.0 copy-start.1
  2.9 1.0 %copy-done.1 = f32[1,8,14336]{2,1,0:T(8,128)S(1)} copy-done((f32[1,8,14336]{2,1,0:T(8,128)S(1)}, f32[1,8,14336]{2,1,0:T(8,128)}, u32[]{:S(2)}) %copy-start.1) | copy-done | bytes 458776
  3.9 0.0 copy-start.3
  3.9 0.9 %copy-done.3 = bf16[1,8,14336]{2,1,0:T(8,128)(2,1)S(1)} copy-done((bf16[1,8,14336]{2,1,0:T(8,128)(2,1)S(1)}, bf16[1,8,14336]{2,1,0:T(8,128)(2,1)}, u32[]{:S(2)}) %copy-start.3) | copy-done | bytes 229400
  4.9 0.0 copy-start.4
  4.9 0.8 %copy-done.4 = bf16[64,192]{1,0:T(8,128)(2,1)S(1)} copy-done((bf16[64,192]{1,0:T(8,128)(2,1)S(1)}, bf16[64,192]{1,0:T(8,128)(2,1)}, u32[]{:S(2)}) %copy-start.4) | copy-done | bytes 24600
  5.6 43.4 %shard_map.77 = (f32[8,14336]{1,0:T(8,128)S(1)}, f32[448,256]{1,0:T(8,128)S(1)}) custom-call(f32[8,14336]{1,0:T(8,128)S(1)} %bitcast.5, bf16[8,14336]{1,0:T(8,128)(2,1)S(1)} %bitcast.8, s32[128,224]{1,0:T(8,128)S(1)} %reshape.7.sel_ref, bf16[2,512,512]{2,1,0:T(8,128)(2,1)S(1)} %copy-done, bf16[8,128,16]{2,1,0:T(8,128)(2,1)S(1)} %copy-done.2, ...), custom_call_target="tpu_custom_call" | custom-call | tf_op jit(solution)/shard_map/pallas_call | solution.py:325
  49.1 0.8 %copy.10 = f32[1,8,14336]{2,1,0:T(8,128)} copy(f32[1,8,14336]{2,1,0:T(8,128)S(1)} %bitcast.7) | data formatting | bytes 917504
  49.8 0.8 %copy.11 = f32[256,448]{0,1:T(8,128)} copy(f32[256,448]{0,1:T(8,128)S(1)} %bitcast.6) | data formatting | bytes 917504
Async XLA Ops:
  0.6 1.1 %copy-start.2 = (bf16[8,128,16]{2,1,0:T(8,128)(2,1)S(1)}, bf16[8,128,16]{2,1,0:T(8,128)(2,1)}, u32[]{:S(2)}) copy-start(bf16[8,128,16]{2,1,0:T(8,128)(2,1)} %constant.7.clone.rows_hbm) | copy-start | bytes 98308
  1.7 1.2 %copy-start = (bf16[2,512,512]{2,1,0:T(8,128)(2,1)S(1)}, bf16[2,512,512]{2,1,0:T(8,128)(2,1)}, u32[]{:S(2)}) copy-start(bf16[2,512,512]{2,1,0:T(8,128)(2,1)} %constant.6.clone.spread_hbm) | copy-start | bytes 3145732
  2.9 1.0 %copy-start.1 = (f32[1,8,14336]{2,1,0:T(8,128)S(1)}, f32[1,8,14336]{2,1,0:T(8,128)}, u32[]{:S(2)}) copy-start(f32[1,8,14336]{2,1,0:T(8,128)} %param.6) | copy-start | bytes 1376260
  3.9 0.9 %copy-start.3 = (bf16[1,8,14336]{2,1,0:T(8,128)(2,1)S(1)}, bf16[1,8,14336]{2,1,0:T(8,128)(2,1)}, u32[]{:S(2)}) copy-start(bf16[1,8,14336]{2,1,0:T(8,128)(2,1)} %param.7) | copy-start | bytes 688132
  4.9 0.8 %copy-start.4 = (bf16[64,192]{1,0:T(8,128)(2,1)S(1)}, bf16[64,192]{1,0:T(8,128)(2,1)}, u32[]{:S(2)}) copy-start(bf16[64,192]{1,0:T(8,128)(2,1)} %constant.8.clone.inv_ref) | copy-start | bytes 73732

commit v2 on v1

v2 whole, which is shorter than its diff:
```python
import functools

import jax
import jax.numpy as jnp
import numpy as np
from jax import lax
from jax.experimental import pallas as pl
from jax.experimental.pallas import tpu as pltpu
from jax.sharding import PartitionSpec as P

SIDE = 64
BLOCK = 8
MESH = pl.DeviceIdType.MESH
F32 = jnp.float32
BF16 = jnp.bfloat16


def cosine_table():
    freq = np.arange(SIDE, dtype=np.float64)[:, None]
    place = np.arange(SIDE, dtype=np.float64)[None, :]
    scale = np.where(freq == 0, np.sqrt(1.0 / SIDE), np.sqrt(2.0 / SIDE))
    return scale * np.cos(np.pi * (2.0 * place + 1.0) * freq / (2.0 * SIDE))


def halves_np(value):
    value = value.astype(np.float32)
    high = value.astype(BF16)
    low = (value - high.astype(np.float32)).astype(BF16)
    return high, low


def tables(spans, devices_z):
    table = cosine_table()
    spread = np.zeros((8 * SIDE, 8, 8, BLOCK))
    for s in range(spans):
        spread[s * SIDE:(s + 1) * SIDE, :, s, :] = table.T.reshape(SIDE, 8, BLOCK)
    spread = np.stack(halves_np(spread.reshape(8 * SIDE, 8 * SIDE)))
    cube = table.reshape(8, BLOCK, devices_z, 8)
    by_a = cube.transpose(2, 3, 1, 0).reshape(devices_z, 64, 8)
    by_u = cube.transpose(2, 1, 3, 0).reshape(devices_z, 64, 8)
    rows = np.concatenate([by_a, by_u], axis=1)
    rows = np.concatenate(halves_np(rows), axis=-1)
    high, low = halves_np(table.T)
    inverse = np.concatenate([high, high, low], axis=1)
    return spread, rows, inverse


def halves(value):
    high = value.astype(BF16)
    low = (value - high.astype(F32)).astype(BF16)
    return high, low


def dot(a, b):
    return jnp.dot(a, b, preferred_element_type=F32)


def dot_t(a, b):
    return lax.dot_general(a, b, (((1,), (1,)), ((), ())), preferred_element_type=F32)


def kernel(
    nx, nz, nq, spans,
    mom_hbm, grad_hbm, sel_hbm, spread_hbm, spread_t_hbm, rows_hbm, inv_hbm,
    res_ref, upd_ref,
    mom, grad, sel, sel_own, spread, spread_t, rows, inv, decayed, lhs, blk, blk_q, numbers, weights, weights_t,
    part, arrived, full, gathered, sums,
    load_sem, part_send, part_sem, full_send, full_sem, plane_send, plane_sem, upd_send, upd_sem,
):
    replica = lax.axis_index("replica")
    fsdp = lax.axis_index("fsdp")
    x, z = fsdp // nz, lax.rem(fsdp, nz)
    y, core = replica // 2, lax.rem(replica, 2)
    ny = nq // 2
    sibling = replica + 1 - 2 * core
    per_core = nx // 2
    core_to, row_to = x // per_core, lax.rem(x, per_core)
    keeps_own = core == core_to
    width = spans * SIDE
    owners = nx * nz
    all_cols = owners * spans

    def outward(n):
        return sorted(range(n), key=lambda d: -min(d, n - d))

    barrier = pltpu.get_barrier_semaphore()
    for dy in outward(ny):
        for c in range(2):
            q = 2 * lax.rem(y + dy, ny) + c
            for r in range(per_core):
                xs = per_core * core + r
                greet = functools.partial(
                    pl.semaphore_signal, barrier, inc=1, device_id=(q, xs * nz + z), device_id_type=MESH
                )
                if dy == 0:
                    pl.when(jnp.logical_or(q != replica, xs != x))(greet)
                else:
                    greet()
    for d in outward(nz)[:-1]:
        peer = x * nz + lax.rem(z + d, nz)
        pl.semaphore_signal(barrier, inc=1, device_id=(replica, peer), device_id_type=MESH)
    pl.semaphore_signal(barrier, inc=1, device_id=(sibling, fsdp), device_id_type=MESH)

    loads = [
        pltpu.make_async_copy(source, target, load_sem.at[n])
        for n, (source, target) in enumerate((
            (sel_hbm.at[replica, x], sel_own), (rows_hbm.at[z], rows), (mom_hbm, mom), (grad_hbm, grad),
            (spread_hbm, spread), (sel_hbm, sel), (spread_t_hbm, spread_t), (inv_hbm, inv),
        ))
    ]
    for load in loads:
        load.start()

    half = lax.broadcasted_iota(jnp.int32, (8, 128), 1) // 64
    sub16 = lax.broadcasted_iota(jnp.int32, (16, 128), 0) & 7

    col = lax.broadcasted_iota(jnp.int32, (owners, all_cols), 1)
    row = lax.broadcasted_iota(jnp.int32, (owners, all_cols), 0) * spans
    inside = jnp.logical_and(col >= row, col < row + spans)
    c_f = lax.broadcasted_iota(jnp.int32, (all_cols, 128), 0).astype(F32)
    c_mod = c_f - spans * jnp.floor((c_f + 0.5) * (1.0 / spans))
    l_i = lax.broadcasted_iota(jnp.int32, (all_cols, 128), 1)
    same_span = c_mod == ((l_i & 63) // 8).astype(F32)
    loads[0].wait()
    placed = None
    for k in range(2):
        left = jnp.where(inside, jnp.broadcast_to(sel_own[k:k + 1, :], (owners, all_cols)), 0).astype(F32)
        right = jnp.where(jnp.logical_and(same_span, l_i // 64 == k), 1.0, 0.0)
        term = dot(left.astype(BF16), right.astype(BF16))
        placed = term if placed is None else placed + term
    blk[...] = placed.astype(jnp.int32)

    def one_hot(f):
        ones = []
        for g in (f, f + 1):
            i_sel = jnp.broadcast_to(blk[g:g + 1, :], (16, 128)) // 8
            ones.append(jnp.where(i_sel == sub16, 1.0, 0.0).astype(BF16))
        return jnp.concatenate(ones, axis=1)

    loads[1].wait()
    for f in range(0, owners, 2):
        weights[:, f * 128:(f + 2) * 128] = dot(rows[:64, :], one_hot(f))

    loads[2].wait()
    loads[3].wait()
    decayed[...] = 0.9 * mom[...] + grad[...].astype(F32)

    def selected(f):
        both = jnp.broadcast_to(blk[f:f + 1, :], (8, 128)) & 7
        return both, pltpu.roll(both, 64, 1)

    def span_columns(zt, xt):
        base = (xt * nz + zt) // 2 * 2 * width
        if zt % 2 == 0:
            return decayed[:, base:base + 8 * SIDE]
        return pltpu.roll(decayed[:, base + width - SIDE:base + 2 * width], 8 * SIDE - SIDE, 1)

    def send_part(zt):
        pltpu.make_async_remote_copy(
            part.at[zt], arrived.at[lax.rem(z - zt + nz, nz) - 1], part_send, part_sem,
            device_id=(replica, x * nz + zt), device_id_type=MESH,
        ).start()

    tall = owners * 8 // 2
    for group in range(2):
        for zt in range(group * nz // 2, (group + 1) * nz // 2):
            for xt in range(0, nx, 2):
                at = zt * nx * 8 + xt * 8
                high, low = halves(jnp.concatenate([span_columns(zt, xt), span_columns(zt, xt + 1)], axis=0))
                lhs[0, at:at + 16, :] = high
                lhs[1, at:at + 16, :] = low
        if group == 0:
            loads[4].wait()
        at = slice(group * tall, (group + 1) * tall)
        coeff = dot(lhs[0, at, :], spread[0]) + dot(lhs[1, at, :], spread[0]) + dot(lhs[0, at, :], spread[1])
        for g in range(tall // 8):
            zt, xt = group * nz // 2 + g // nx, g % nx
            f = xt * nz + zt
            j_own, j_other = selected(f)
            direct = other = jnp.zeros((8, 128), F32)
            for t in range(4):
                piece = coeff[8 * g:8 * g + 8, 128 * t:128 * t + 128]
                direct = jnp.where(j_own // 2 == t, piece, direct)
                other = jnp.where(j_other // 2 == t, piece, other)
            picked = jnp.where((j_own & 1) == half, direct, pltpu.roll(other, 64, 1))
            total = None
            for a in range(8):
                term = weights[8 * a:8 * a + 8, f * 128:f * 128 + 128] * jnp.broadcast_to(picked[a:a + 1, :], (8, 128))
                total = term if total is None else total + term
            part[zt, xt] = total
        if group == 0:
            pl.semaphore_wait(barrier, nz - 1 + nx * ny - jnp.where(keeps_own, 1, 0) + 1)
        for zt in range(group * nz // 2, (group + 1) * nz // 2):
            pl.when(z != zt)(functools.partial(send_part, zt))

    for f in range(0, owners, 2):
        weights_t[:, f * 128:(f + 2) * 128] = dot(rows[64:, :], one_hot(f))
    loads[5].wait()
    c_own = lax.broadcasted_iota(jnp.int32, (all_cols, 128), 0) - spans * fsdp
    s_own = (lax.broadcasted_iota(jnp.int32, (all_cols, 128), 1) & 63) // 8
    pick = jnp.where(jnp.logical_and(c_own == s_own, s_own < spans), 1.0, 0.0).astype(BF16)
    blk_q[...] = dot(sel[...].reshape(nq * nx * 2, all_cols).astype(F32).astype(BF16), pick).astype(jnp.int32)

    around = sorted(range(ny), key=lambda d: (min(d, ny - d), d))
    tiles = [(d, c, r) for d in around for c in range(2) for r in range(per_core)]
    reach = [[n for n, (d, _, _) in enumerate(tiles) if min(d, ny - d) == g] for g in range(ny // 2 + 1)]
    row_half = half[:1]
    for n, (d, c, r) in enumerate(tiles):
        at = ((2 * lax.rem(y + d, ny) + c) * nx + per_core * core + r) * 2
        pair = jnp.where(row_half == 0, blk_q[pl.ds(at, 1), :], blk_q[pl.ds(at + 1, 1), :])
        numbers[0, n:n + 1, :] = pair
        numbers[1, n:n + 1, :] = pltpu.roll(pair, 64, 1)

    pltpu.make_async_copy(arrived, arrived, part_sem).wait()
    for xt in range(nx):
        total = part[z, xt]
        for d in range(nz - 1):
            total = total + arrived[d, xt]
        full[z, xt] = total

    for d in outward(nz)[:-1]:
        pltpu.make_async_remote_copy(
            full.at[z], full.at[z], full_send, full_sem,
            device_id=(replica, x * nz + lax.rem(z + d, nz)), device_id_type=MESH,
        ).start()

    def send_plane(dx, dy):
        xt = lax.rem(x + dx, nx)
        slot = around.index((ny - dy) % ny) * 2 * per_core + core * per_core + row_to
        pltpu.make_async_remote_copy(
            full.at[z, xt], gathered.at[slot], plane_send, plane_sem.at[min(dy, ny - dy)],
            device_id=(2 * lax.rem(y + dy, ny) + core_to, xt * nz + z), device_id_type=MESH,
        ).start()

    targets = [(dx, dy) for dx in range(nx) for dy in range(ny)]
    for dx, dy in sorted(targets, key=lambda t: -min(t[0], nx - t[0]) - min(t[1], ny - t[1])):
        send = functools.partial(send_plane, dx, dy)
        if dx == dy == 0:
            pl.when(jnp.logical_not(keeps_own))(send)
        else:
            send()

    @pl.when(keeps_own)
    def _():
        gathered[core * per_core + row_to] = full[z, x]

    def await_tiles(first, count, sem):
        ref = gathered.at[pl.ds(first, count)]
        pltpu.make_async_copy(ref, ref, sem).wait()

    def gather_group(g):
        slots = reach[g]
        if g == 0:
            pl.when(keeps_own)(lambda: await_tiles(1, len(slots) - 1, plane_sem.at[0]))
            pl.when(jnp.logical_not(keeps_own))(lambda: await_tiles(0, len(slots), plane_sem.at[0]))
        else:
            await_tiles(slots[0], len(slots), plane_sem.at[g])
        for r in range(per_core):
            mine = [n for n in slots if tiles[n][2] == r]
            values = [gathered[n] for n in mine]
            others = [pltpu.roll(value, 64, 1) for value in values]
            here = [jnp.broadcast_to(numbers[0, n:n + 1, :], (8, 128)) for n in mine]
            there = [jnp.broadcast_to(numbers[1, n:n + 1, :], (8, 128)) for n in mine]
            for t in range(4):
                j_t = 2 * t + half
                i_here = [jnp.where((b & 7) == j_t, b // 8, -1) for b in here]
                i_there = [jnp.where((b & 7) == j_t, b // 8, -1) for b in there]
                for i in range(8):
                    at = (slice(8 * i, 8 * i + 8), slice(128 * t, 128 * t + 128))
                    total = None if g == 0 else sums[r, at[0], at[1]]
                    for value, other, h, o in zip(values, others, i_here, i_there):
                        term = jnp.where(h == i, value, jnp.where(o == i, other, 0.0))
                        total = term if total is None else total + term
                    sums[r, at[0], at[1]] = total

    gather_group(0)
    gather_group(1)

    loads[6].wait()
    pltpu.make_async_copy(full.at[pl.ds(0, nz - 1)], full.at[pl.ds(0, nz - 1)], full_sem).wait()
    for p in range(owners // 2):
        parts = []
        for f in (2 * p, 2 * p + 1):
            j_own, j_other = selected(f)
            total = None
            for u in range(8):
                term = weights_t[8 * u:8 * u + 8, f * 128:f * 128 + 128] * jnp.broadcast_to(
                    full[f % nz, f // nz, u:u + 1, :], (8, 128)
                )
                total = term if total is None else total + term
            other = pltpu.roll(total, 64, 1)
            parts.append(jnp.concatenate([
                jnp.where(j_own == 2 * t + half, total, 0.0) + jnp.where(j_other == 2 * t + half, other, 0.0)
                for t in range(4)
            ], axis=1))
        high, low = halves(jnp.concatenate(parts, axis=0))
        lhs[0, 16 * p:16 * p + 16, :] = high
        lhs[1, 16 * p:16 * p + 16, :] = low
    for m in range(2):
        at = slice(m * tall, (m + 1) * tall)
        space = dot(lhs[0, at, :], spread_t[0]) + dot(lhs[1, at, :], spread_t[0]) + dot(lhs[0, at, :], spread_t[1])
        for g in range(0, tall // 8, 2):
            f = m * (tall // 8) + g
            pair = jnp.concatenate([space[8 * g:8 * g + 8, :width], space[8 * g + 8:8 * g + 16, :width]], axis=1)
            at_cols = slice(f * width, (f + 2) * width)
            res_ref[:, at_cols] = decayed[:, at_cols] - pair

    for g in range(2, len(reach)):
        gather_group(g)

    loads[7].wait()
    spatial = []
    for r in range(per_core):
        high, low = halves(sums[r])
        spatial.append(dot(inv[...], jnp.concatenate([high, low, high], axis=0)))
    high, low = halves(jnp.concatenate(spatial, axis=0))
    both = jnp.concatenate([high, low], axis=0)
    lanes = per_core * SIDE
    mine = pl.ds(pl.multiple_of(core * lanes, lanes), lanes)
    pieces = []
    tall = width // 2
    for m in range(2):
        at = slice(m * tall, (m + 1) * tall)
        wide = dot_t(spread[0, at, :], both)
        upd_ref[at, mine] = wide[:, :lanes] + wide[:, lanes:] + dot_t(spread[1, at, :], high)
        place = upd_ref.at[at, mine]
        piece = pltpu.make_async_remote_copy(
            place, place, upd_send.at[m], upd_sem.at[m], device_id=(sibling, fsdp), device_id_type=MESH
        )
        piece.start()
        pieces.append(piece)

    seven = full.at[pl.ds(0, nz - 1)]
    pltpu.make_async_copy(seven, seven, part_send).wait()
    pltpu.make_async_copy(seven, seven, full_send).wait()
    pl.when(keeps_own)(lambda: await_tiles(1, len(tiles) - 1, plane_send))
    pl.when(jnp.logical_not(keeps_own))(lambda: await_tiles(0, len(tiles), plane_send))
    for piece in pieces:
        piece.wait()


def local(nx, nz, nq, momentum, gradient, selection):
    rows_dev, all_width = momentum.shape[1:]
    owners = nx * nz
    width = all_width // owners
    spans = width // SIDE
    spread, rows, inverse = tables(spans, nz)
    sel = selection.transpose(0, 1, 3, 2)
    spread_t = spread.transpose(0, 2, 1)
    per_core = nx // 2
    hbm = pl.BlockSpec(memory_space=pltpu.HBM)
    vmem = pl.BlockSpec(memory_space=pltpu.VMEM)
    dma = pltpu.SemaphoreType.DMA
    slab = (rows_dev, all_width)
    res, upd = pl.pallas_call(
        functools.partial(kernel, nx, nz, nq, spans),
        out_shape=(
            jax.ShapeDtypeStruct(slab, F32),
            jax.ShapeDtypeStruct((width, nx * SIDE), F32),
        ),
        in_specs=[hbm] * 7,
        out_specs=(vmem, vmem),
        scratch_shapes=[
            pltpu.VMEM(slab, F32),
            pltpu.VMEM(slab, BF16),
            pltpu.VMEM(sel.shape, jnp.int32),
            pltpu.VMEM(sel.shape[2:], jnp.int32),
            pltpu.VMEM(spread.shape, BF16),
            pltpu.VMEM(spread.shape, BF16),
            pltpu.VMEM(rows.shape[1:], BF16),
            pltpu.VMEM(inverse.shape, BF16),
            pltpu.VMEM(slab, F32),
            pltpu.VMEM((2, owners * 8, 8 * SIDE), BF16),
            pltpu.VMEM((owners, 128), jnp.int32),
            pltpu.VMEM((nq * nx * 2, 128), jnp.int32),
            pltpu.VMEM((2, nq * per_core, 128), jnp.int32),
            pltpu.VMEM((64, owners * 128), F32),
            pltpu.VMEM((64, owners * 128), F32),
            pltpu.VMEM((nz, nx, 8, 128), F32),
            pltpu.VMEM((nz - 1, nx, 8, 128), F32),
            pltpu.VMEM((nz, nx, 8, 128), F32),
            pltpu.VMEM((nq * per_core, 8, 128), F32),
            pltpu.VMEM((per_core, SIDE, 8 * SIDE), F32),
            dma((8,)), dma, dma, dma, dma, dma, dma((nq // 4 + 1,)), dma((2,)), dma((2,)),
        ],
        compiler_params=pltpu.CompilerParams(
            collective_id=0, has_side_effects=True, vmem_limit_bytes=62 * 1024 * 1024
        ),
    )(momentum[0], gradient[0], sel, jnp.asarray(spread), jnp.asarray(spread_t), jnp.asarray(rows), jnp.asarray(inverse))
    return res[None], upd.T


def solution(mesh):
    nq = mesh.shape["replica"]
    nz = 8
    nx = mesh.shape["fsdp"] // nz
    return jax.shard_map(
        functools.partial(local, nx, nz, nq),
        mesh=mesh,
        in_specs=(P("replica", "fsdp", None), P("replica", "fsdp", None), P()),
        out_specs=(P("replica", "fsdp", None), P(None, "fsdp")),
        check_vma=False,
    )
```

time: 50.9 us -> 35.6 us (0.70)
  Pallas kernels: 43.4 us -> 32.2 us
  local copies, waits for them, and re-layouts: 6.51 us -> 2.64 us
    pallas_call x1, Pallas kernels: 43.4 us -> 32.2 us  [local(): pl.pallas_call(functools.partial(kernel, nx, nz, nq, spans), out_shape=(j...]
    unnamed x12 -> x4, local copies, waits for them, and re-layouts: 5.48 us -> 2.64 us
    reshape x1 -> x0, local copies, waits for them, and re-layouts: 1.04 us -> none  [local(): sel = selection.transpose(0, 1, 3, 2).reshape(nq * nx * 2, owners * spans)]
where the time goes in v2:
time: 35.6 us; the launch traced here: 35.5 us
  Pallas kernels  32.2 us (90%)
  local copies, waits for them, and re-layouts  2.64 us (7%)
  between operations  0.65 us (2%)
    pallas_call x1, Pallas kernels, local(): pl.pallas_call(functools.partial(kernel, nx, nz, nq, spans), out_shape=(j...  32.2 us
    unnamed x4, local copies, waits for them, and re-layouts  2.64 us

profile of v2, /device:TPU:1, one launch (start us, length us, event | category | flops | bytes accessed | tf_op | source)
XLA Modules:
  0.0 35.5 jit_solution(8353165853092938806)
XLA Ops:
  0.6 32.2 %shard_map.86 = (f32[8,14336]{1,0:T(8,128)}, f32[448,256]{1,0:T(8,128)}) custom-call(f32[8,14336]{1,0:T(8,128)} %bitcast.5, bf16[8,14336]{1,0:T(8,128)(2,1)} %bitcast.8, s32[16,4,2,224]{3,2,1,0:T(2,128)} %bitcast.9, bf16[2,512,512]{2,1,0:T(8,128)(2,1)} %constant.8.clone.spread_hbm, bf16[2,512,512]{2,1,0:T(8,128)(2,1)} %constant.9.clone.spread_t_hbm, ...), custom_call_target="tpu_custom_call" | custom-call | tf_op jit(solution)/shard_map/pallas_call | solution.py:355
  32.8 0.0 copy-start
  32.8 1.9 %copy.11 = f32[1,8,14336]{2,1,0:T(8,128)} copy(f32[1,8,14336]{2,1,0:T(8,128)} %bitcast.7) | data formatting | bytes 917504
  34.7 0.0 copy-done
  34.7 0.8 %copy.12 = f32[256,448]{0,1:T(8,128)} copy(f32[256,448]{0,1:T(8,128)S(1)} %bitcast.6) | data formatting | bytes 917504
Async XLA Ops:
  32.8 1.9 %copy-start = (f32[448,256]{1,0:T(8,128)S(1)}, f32[448,256]{1,0:T(8,128)}, u32[]{:S(2)}) copy-start(f32[448,256]{1,0:T(8,128)} %get-tuple-element.5) | copy-start | bytes 1376260

commit v3 on v2

--- a/solution.py
+++ b/solution.py
@@ -84,6 +84,9 @@
         return sorted(range(n), key=lambda d: -min(d, n - d))
 
     barrier = pltpu.get_barrier_semaphore()
+    for d in outward(nz)[:-1]:
+        peer = x * nz + lax.rem(z + d, nz)
+        pl.semaphore_signal(barrier, inc=1, device_id=(replica, peer), device_id_type=MESH)
     for dy in outward(ny):
         for c in range(2):
             q = 2 * lax.rem(y + dy, ny) + c
@@ -96,9 +99,6 @@
                     pl.when(jnp.logical_or(q != replica, xs != x))(greet)
                 else:
                     greet()
-    for d in outward(nz)[:-1]:
-        peer = x * nz + lax.rem(z + d, nz)
-        pl.semaphore_signal(barrier, inc=1, device_id=(replica, peer), device_id_type=MESH)
     pl.semaphore_signal(barrier, inc=1, device_id=(sibling, fsdp), device_id_type=MESH)
 
     loads = [
@@ -108,7 +108,7 @@
             (spread_hbm, spread), (sel_hbm, sel), (spread_t_hbm, spread_t), (inv_hbm, inv),
         ))
     ]
-    for load in loads:
+    for load in loads[:5]:
         load.start()
 
     half = lax.broadcasted_iota(jnp.int32, (8, 128), 1) // 64
@@ -193,6 +193,9 @@
         for zt in range(group * nz // 2, (group + 1) * nz // 2):
             pl.when(z != zt)(functools.partial(send_part, zt))
 
+    for load in loads[5:]:
+        load.start()
+
     for f in range(0, owners, 2):
         weights_t[:, f * 128:(f + 2) * 128] = dot(rows[64:, :], one_hot(f))
     loads[5].wait()
@@ -339,6 +342,17 @@
         piece.wait()
 
 
+def store_kernel(res_vmem, upd_vmem, res_ref, upd_ref, sems):
+    stores = [
+        pltpu.make_async_copy(source, target, sems.at[n])
+        for n, (source, target) in enumerate(((res_vmem, res_ref), (upd_vmem, upd_ref)))
+    ]
+    for store in stores:
+        store.start()
+    for store in stores:
+        store.wait()
+
+
 def local(nx, nz, nq, momentum, gradient, selection):
     rows_dev, all_width = momentum.shape[1:]
     owners = nx * nz
@@ -352,11 +366,12 @@
     vmem = pl.BlockSpec(memory_space=pltpu.VMEM)
     dma = pltpu.SemaphoreType.DMA
     slab = (rows_dev, all_width)
+    operands = (momentum[0], gradient[0], sel, *map(jnp.asarray, (spread, spread_t, rows, inverse)))
     res, upd = pl.pallas_call(
         functools.partial(kernel, nx, nz, nq, spans),
         out_shape=(
-            jax.ShapeDtypeStruct(slab, F32),
-            jax.ShapeDtypeStruct((width, nx * SIDE), F32),
+            pltpu.VMEM(slab, F32),
+            pltpu.VMEM((width, nx * SIDE), F32),
         ),
         in_specs=[hbm] * 7,
         out_specs=(vmem, vmem),
@@ -384,9 +399,17 @@
             dma((8,)), dma, dma, dma, dma, dma, dma((nq // 4 + 1,)), dma((2,)), dma((2,)),
         ],
         compiler_params=pltpu.CompilerParams(
-            collective_id=0, has_side_effects=True, vmem_limit_bytes=62 * 1024 * 1024
+            collective_id=0, has_side_effects=True, vmem_limit_bytes=24 * 1024 * 1024
         ),
-    )(momentum[0], gradient[0], sel, jnp.asarray(spread), jnp.asarray(spread_t), jnp.asarray(rows), jnp.asarray(inverse))
+    )(*(pltpu.with_memory_space_constraint(array, pltpu.HBM) for array in operands))
+    res, upd = pl.pallas_call(
+        store_kernel,
+        out_shape=(jax.ShapeDtypeStruct(slab, F32), jax.ShapeDtypeStruct(upd.shape, F32)),
+        in_specs=[vmem] * 2,
+        out_specs=(hbm, hbm),
+        scratch_shapes=[dma((2,))],
+        compiler_params=pltpu.CompilerParams(vmem_limit_bytes=4 * 1024 * 1024),
+    )(*(pltpu.with_memory_space_constraint(array, pltpu.VMEM) for array in (res, upd)))
     return res[None], upd.T
 
 

time: 35.6 us -> 33.1 us (0.930)
  local copies, waits for them, and re-layouts: 2.64 us -> 0 us
    unnamed x4 -> x0, local copies, waits for them, and re-layouts: 2.64 us -> none
    pallas_call x1 -> x2, Pallas kernels: 32.2 us -> 32.3 us  [the longest x1 31.3 us: local(): pl.pallas_call(functools.partial(kernel, nx, nz, nq, spans), out_shape=(p...]
where the time goes in v3:
time: 33.1 us; the launch traced here: 32.9 us
  Pallas kernels  32.3 us (98%)
  between operations  0.64 us (2%)
    pallas_call x1, Pallas kernels, local(): pl.pallas_call(functools.partial(kernel, nx, nz, nq, spans), out_shape=(p...  31.3 us
    pallas_call x1, Pallas kernels, local(): pl.pallas_call(store_kernel, out_shape=(jax.ShapeDtypeStruct(slab, F32),...  0.94 us

profile of v3, /device:TPU:1, one launch (start us, length us, event | category | flops | bytes accessed | tf_op | source)
XLA Modules:
  0.0 32.9 jit_solution(1986136164509830831)
XLA Ops:
  0.6 31.3 %shard_map.86 = (f32[8,14336]{1,0:T(8,128)S(1)}, f32[448,256]{1,0:T(8,128)S(1)}) custom-call(f32[8,14336]{1,0:T(8,128)} %bitcast.5, bf16[8,14336]{1,0:T(8,128)(2,1)} %bitcast.6, s32[16,4,2,224]{3,2,1,0:T(2,128)} %bitcast.7, bf16[2,512,512]{2,1,0:T(8,128)(2,1)} %constant.8.clone.spread_hbm, bf16[2,512,512]{2,1,0:T(8,128)(2,1)} %constant.9.clone.spread_t_hbm, ...), custom_call_target="tpu_custom_call" | custom-call | tf_op jit(solution)/shard_map/pallas_call | solution.py:370
  32.0 0.9 %shard_map.87 = (f32[8,14336]{1,0:T(8,128)}, f32[448,256]{1,0:T(8,128)}) custom-call(f32[8,14336]{1,0:T(8,128)S(1)} %get-tuple-element.6.res_vmem, f32[448,256]{1,0:T(8,128)S(1)} %get-tuple-element.7.upd_vmem), custom_call_target="tpu_custom_call" | custom-call | tf_op jit(solution)/shard_map/pallas_call | solution.py:405

commit v4 on v3

--- a/solution.py
+++ b/solution.py
@@ -40,8 +40,8 @@
     by_u = cube.transpose(2, 1, 3, 0).reshape(devices_z, 64, 8)
     rows = np.concatenate([by_a, by_u], axis=1)
     rows = np.concatenate(halves_np(rows), axis=-1)
-    high, low = halves_np(table.T)
-    inverse = np.concatenate([high, high, low], axis=1)
+    high, low = halves_np(np.kron(np.eye(2), table))
+    inverse = np.concatenate([high, high, low], axis=0)
     return spread, rows, inverse
 
 
@@ -53,10 +53,6 @@
 
 def dot(a, b):
     return jnp.dot(a, b, preferred_element_type=F32)
-
-
-def dot_t(a, b):
-    return lax.dot_general(a, b, (((1,), (1,)), ((), ())), preferred_element_type=F32)
 
 
 def kernel(
@@ -155,22 +151,15 @@
             return decayed[:, base:base + 8 * SIDE]
         return pltpu.roll(decayed[:, base + width - SIDE:base + 2 * width], 8 * SIDE - SIDE, 1)
 
-    def send_part(zt):
-        pltpu.make_async_remote_copy(
-            part.at[zt], arrived.at[lax.rem(z - zt + nz, nz) - 1], part_send, part_sem,
-            device_id=(replica, x * nz + zt), device_id_type=MESH,
-        ).start()
-
+    for zt in range(nz):
+        for xt in range(0, nx, 2):
+            at = zt * nx * 8 + xt * 8
+            high, low = halves(jnp.concatenate([span_columns(zt, xt), span_columns(zt, xt + 1)], axis=0))
+            lhs[0, at:at + 16, :] = high
+            lhs[1, at:at + 16, :] = low
+    loads[4].wait()
     tall = owners * 8 // 2
     for group in range(2):
-        for zt in range(group * nz // 2, (group + 1) * nz // 2):
-            for xt in range(0, nx, 2):
-                at = zt * nx * 8 + xt * 8
-                high, low = halves(jnp.concatenate([span_columns(zt, xt), span_columns(zt, xt + 1)], axis=0))
-                lhs[0, at:at + 16, :] = high
-                lhs[1, at:at + 16, :] = low
-        if group == 0:
-            loads[4].wait()
         at = slice(group * tall, (group + 1) * tall)
         coeff = dot(lhs[0, at, :], spread[0]) + dot(lhs[1, at, :], spread[0]) + dot(lhs[0, at, :], spread[1])
         for g in range(tall // 8):
@@ -188,10 +177,13 @@
                 term = weights[8 * a:8 * a + 8, f * 128:f * 128 + 128] * jnp.broadcast_to(picked[a:a + 1, :], (8, 128))
                 total = term if total is None else total + term
             part[zt, xt] = total
-        if group == 0:
-            pl.semaphore_wait(barrier, nz - 1 + nx * ny - jnp.where(keeps_own, 1, 0) + 1)
-        for zt in range(group * nz // 2, (group + 1) * nz // 2):
-            pl.when(z != zt)(functools.partial(send_part, zt))
+    pl.semaphore_wait(barrier, nz - 1 + nx * ny - jnp.where(keeps_own, 1, 0) + 1)
+    for d in outward(nz)[:-1]:
+        zt = lax.rem(z + d, nz)
+        pltpu.make_async_remote_copy(
+            part.at[zt], arrived.at[nz - d - 1], part_send, part_sem,
+            device_id=(replica, x * nz + zt), device_id_type=MESH,
+        ).start()
 
     for load in loads[5:]:
         load.start()
@@ -276,10 +268,29 @@
                         total = term if total is None else total + term
                     sums[r, at[0], at[1]] = total
 
-    gather_group(0)
-    gather_group(1)
+    for g in range(len(reach)):
+        gather_group(g)
 
     loads[6].wait()
+    loads[7].wait()
+    high, low = halves(jnp.concatenate([sums[r] for r in range(per_core)], axis=0))
+    across = dot(high, spread_t[0]) + dot(low, spread_t[0]) + dot(high, spread_t[1])
+    high, low = halves(across.T)
+    stacked = jnp.concatenate([high, low, high], axis=1)
+    lanes = per_core * SIDE
+    mine = pl.ds(pl.multiple_of(core * lanes, lanes), lanes)
+    pieces = []
+    strip = width // 2
+    for m in range(2):
+        at = slice(m * strip, (m + 1) * strip)
+        upd_ref[at, mine] = dot(stacked[at, :], inv[...])
+        place = upd_ref.at[at, mine]
+        piece = pltpu.make_async_remote_copy(
+            place, place, upd_send.at[m], upd_sem.at[m], device_id=(sibling, fsdp), device_id_type=MESH
+        )
+        piece.start()
+        pieces.append(piece)
+
     pltpu.make_async_copy(full.at[pl.ds(0, nz - 1)], full.at[pl.ds(0, nz - 1)], full_sem).wait()
     for p in range(owners // 2):
         parts = []
@@ -307,31 +318,6 @@
             pair = jnp.concatenate([space[8 * g:8 * g + 8, :width], space[8 * g + 8:8 * g + 16, :width]], axis=1)
             at_cols = slice(f * width, (f + 2) * width)
             res_ref[:, at_cols] = decayed[:, at_cols] - pair
-
-    for g in range(2, len(reach)):
-        gather_group(g)
-
-    loads[7].wait()
-    spatial = []
-    for r in range(per_core):
-        high, low = halves(sums[r])
-        spatial.append(dot(inv[...], jnp.concatenate([high, low, high], axis=0)))
-    high, low = halves(jnp.concatenate(spatial, axis=0))
-    both = jnp.concatenate([high, low], axis=0)
-    lanes = per_core * SIDE
-    mine = pl.ds(pl.multiple_of(core * lanes, lanes), lanes)
-    pieces = []
-    tall = width // 2
-    for m in range(2):
-        at = slice(m * tall, (m + 1) * tall)
-        wide = dot_t(spread[0, at, :], both)
-        upd_ref[at, mine] = wide[:, :lanes] + wide[:, lanes:] + dot_t(spread[1, at, :], high)
-        place = upd_ref.at[at, mine]
-        piece = pltpu.make_async_remote_copy(
-            place, place, upd_send.at[m], upd_sem.at[m], device_id=(sibling, fsdp), device_id_type=MESH
-        )
-        piece.start()
-        pieces.append(piece)
 
     seven = full.at[pl.ds(0, nz - 1)]
     pltpu.make_async_copy(seven, seven, part_send).wait()

time: 33.1 us -> 32.4 us (0.979)
  Pallas kernels: 32.3 us -> 31.6 us
    pallas_call x1, Pallas kernels: 31.3 us -> 30.7 us  [local(): pl.pallas_call(functools.partial(kernel, nx, nz, nq, spans), out_shape=(p...]
where the time goes in v4:
time: 32.4 us; the launch traced here: 32.2 us
  Pallas kernels  31.6 us (98%)
  between operations  0.64 us (2%)
    pallas_call x1, Pallas kernels, local(): pl.pallas_call(functools.partial(kernel, nx, nz, nq, spans), out_shape=(p...  30.7 us
    pallas_call x1, Pallas kernels, local(): pl.pallas_call(store_kernel, out_shape=(jax.ShapeDtypeStruct(slab, F32),...  0.94 us

profile of v4, /device:TPU:1, one launch (start us, length us, event | category | flops | bytes accessed | tf_op | source)
XLA Modules:
  0.0 32.2 jit_solution(13575224881491802528)
XLA Ops:
  0.6 30.7 %shard_map.86 = (f32[8,14336]{1,0:T(8,128)S(1)}, f32[448,256]{1,0:T(8,128)S(1)}) custom-call(f32[8,14336]{1,0:T(8,128)} %bitcast.5, bf16[8,14336]{1,0:T(8,128)(2,1)} %bitcast.6, s32[16,4,2,224]{3,2,1,0:T(2,128)} %bitcast.7, bf16[2,512,512]{2,1,0:T(8,128)(2,1)} %constant.8.clone.spread_hbm, bf16[2,512,512]{2,1,0:T(8,128)(2,1)} %constant.9.clone.spread_t_hbm, ...), custom_call_target="tpu_custom_call" | custom-call | tf_op jit(solution)/shard_map/pallas_call | solution.py:356
  31.3 0.9 %shard_map.87 = (f32[8,14336]{1,0:T(8,128)}, f32[448,256]{1,0:T(8,128)}) custom-call(f32[8,14336]{1,0:T(8,128)S(1)} %get-tuple-element.6.res_vmem, f32[448,256]{1,0:T(8,128)S(1)} %get-tuple-element.7.upd_vmem), custom_call_target="tpu_custom_call" | custom-call | tf_op jit(solution)/shard_map/pallas_call | solution.py:391

commit v5 on v4

--- a/solution.py
+++ b/solution.py
@@ -61,7 +61,7 @@
     res_ref, upd_ref,
     mom, grad, sel, sel_own, spread, spread_t, rows, inv, decayed, lhs, blk, blk_q, numbers, weights, weights_t,
     part, arrived, full, gathered, sums,
-    load_sem, part_send, part_sem, full_send, full_sem, plane_send, plane_sem, upd_send, upd_sem,
+    load_sem, part_send, part_sem, full_send, full_sem, plane_send, plane_sem, upd_send, upd_sem, ready,
 ):
     replica = lax.axis_index("replica")
     fsdp = lax.axis_index("fsdp")
@@ -80,22 +80,25 @@
         return sorted(range(n), key=lambda d: -min(d, n - d))
 
     barrier = pltpu.get_barrier_semaphore()
+    first = replica - core
     for d in outward(nz)[:-1]:
         peer = x * nz + lax.rem(z + d, nz)
-        pl.semaphore_signal(barrier, inc=1, device_id=(replica, peer), device_id_type=MESH)
+        pl.semaphore_signal(barrier, inc=1, device_id=(first, peer), device_id_type=MESH)
+    pl.semaphore_signal(barrier, inc=1, device_id=(sibling, fsdp), device_id_type=MESH)
     for dy in outward(ny):
-        for c in range(2):
-            q = 2 * lax.rem(y + dy, ny) + c
-            for r in range(per_core):
-                xs = per_core * core + r
-                greet = functools.partial(
-                    pl.semaphore_signal, barrier, inc=1, device_id=(q, xs * nz + z), device_id_type=MESH
-                )
-                if dy == 0:
-                    pl.when(jnp.logical_or(q != replica, xs != x))(greet)
-                else:
-                    greet()
-    pl.semaphore_signal(barrier, inc=1, device_id=(sibling, fsdp), device_id_type=MESH)
+        q = 2 * lax.rem(y + dy, ny) + 1
+        for r in range(per_core):
+            xs = per_core * core + r
+            greet = functools.partial(
+                pl.semaphore_signal, barrier, inc=1, device_id=(q, xs * nz + z), device_id_type=MESH
+            )
+            if dy == 0:
+                pl.when(jnp.logical_or(q != replica, xs != x))(greet)
+            else:
+                greet()
+
+    def tell_sibling():
+        pl.semaphore_signal(ready, inc=1, device_id=(sibling, fsdp), device_id_type=MESH)
 
     loads = [
         pltpu.make_async_copy(source, target, load_sem.at[n])
@@ -177,7 +180,16 @@
                 term = weights[8 * a:8 * a + 8, f * 128:f * 128 + 128] * jnp.broadcast_to(picked[a:a + 1, :], (8, 128))
                 total = term if total is None else total + term
             part[zt, xt] = total
-    pl.semaphore_wait(barrier, nz - 1 + nx * ny - jnp.where(keeps_own, 1, 0) + 1)
+
+    @pl.when(core == 0)
+    def _():
+        pl.semaphore_wait(barrier, 2 * (nz - 1) + 1)
+        tell_sibling()
+
+    @pl.when(core == 1)
+    def _():
+        pl.semaphore_wait(ready, 1)
+
     for d in outward(nz)[:-1]:
         zt = lax.rem(z + d, nz)
         pltpu.make_async_remote_copy(
@@ -206,18 +218,22 @@
         numbers[0, n:n + 1, :] = pair
         numbers[1, n:n + 1, :] = pltpu.roll(pair, 64, 1)
 
+    @pl.when(core == 1)
+    def _():
+        pl.semaphore_wait(barrier, nx * ny - jnp.where(keeps_own, 1, 0) + 1)
+        tell_sibling()
+
     pltpu.make_async_copy(arrived, arrived, part_sem).wait()
+
+    @pl.when(core == 0)
+    def _():
+        pl.semaphore_wait(ready, 1)
+
     for xt in range(nx):
         total = part[z, xt]
         for d in range(nz - 1):
             total = total + arrived[d, xt]
         full[z, xt] = total
-
-    for d in outward(nz)[:-1]:
-        pltpu.make_async_remote_copy(
-            full.at[z], full.at[z], full_send, full_sem,
-            device_id=(replica, x * nz + lax.rem(z + d, nz)), device_id_type=MESH,
-        ).start()
 
     def send_plane(dx, dy):
         xt = lax.rem(x + dx, nx)
@@ -234,6 +250,12 @@
             pl.when(jnp.logical_not(keeps_own))(send)
         else:
             send()
+
+    for d in outward(nz)[:-1]:
+        pltpu.make_async_remote_copy(
+            full.at[z], full.at[z], full_send, full_sem,
+            device_id=(replica, x * nz + lax.rem(z + d, nz)), device_id_type=MESH,
+        ).start()
 
     @pl.when(keeps_own)
     def _():
@@ -382,7 +404,7 @@
             pltpu.VMEM((nz, nx, 8, 128), F32),
             pltpu.VMEM((nq * per_core, 8, 128), F32),
             pltpu.VMEM((per_core, SIDE, 8 * SIDE), F32),
-            dma((8,)), dma, dma, dma, dma, dma, dma((nq // 4 + 1,)), dma((2,)), dma((2,)),
+            dma((8,)), dma, dma, dma, dma, dma, dma((nq // 4 + 1,)), dma((2,)), dma((2,)), pltpu.SemaphoreType.REGULAR,
         ],
         compiler_params=pltpu.CompilerParams(
             collective_id=0, has_side_effects=True, vmem_limit_bytes=24 * 1024 * 1024

time: 32.4 us -> 31.2 us (0.963)
  Pallas kernels: 31.6 us -> 30.4 us
    pallas_call x1, Pallas kernels: 30.7 us -> 29.4 us  [local(): pl.pallas_call(functools.partial(kernel, nx, nz, nq, spans), out_shape=(p...]
where the time goes in v5:
time: 31.2 us; the launch traced here: 31 us
  Pallas kernels  30.4 us (97%)
  between operations  0.64 us (2%)
    pallas_call x1, Pallas kernels, local(): pl.pallas_call(functools.partial(kernel, nx, nz, nq, spans), out_shape=(p...  29.4 us
    pallas_call x1, Pallas kernels, local(): pl.pallas_call(store_kernel, out_shape=(jax.ShapeDtypeStruct(slab, F32),...  0.94 us

profile of v5, /device:TPU:1, one launch (start us, length us, event | category | flops | bytes accessed | tf_op | source)
XLA Modules:
  0.0 31.0 jit_solution(1649922910914161000)
XLA Ops:
  0.6 29.4 %shard_map.86 = (f32[8,14336]{1,0:T(8,128)S(1)}, f32[448,256]{1,0:T(8,128)S(1)}) custom-call(f32[8,14336]{1,0:T(8,128)} %bitcast.5, bf16[8,14336]{1,0:T(8,128)(2,1)} %bitcast.6, s32[16,4,2,224]{3,2,1,0:T(2,128)} %bitcast.7, bf16[2,512,512]{2,1,0:T(8,128)(2,1)} %constant.8.clone.spread_hbm, bf16[2,512,512]{2,1,0:T(8,128)(2,1)} %constant.9.clone.spread_t_hbm, ...), custom_call_target="tpu_custom_call" | custom-call | tf_op jit(solution)/shard_map/pallas_call | solution.py:378
  30.1 0.9 %shard_map.87 = (f32[8,14336]{1,0:T(8,128)}, f32[448,256]{1,0:T(8,128)}) custom-call(f32[8,14336]{1,0:T(8,128)S(1)} %get-tuple-element.6.res_vmem, f32[448,256]{1,0:T(8,128)S(1)} %get-tuple-element.7.upd_vmem), custom_call_target="tpu_custom_call" | custom-call | tf_op jit(solution)/shard_map/pallas_call | solution.py:413

commit v6 on v5

--- a/solution.py
+++ b/solution.py
@@ -59,7 +59,7 @@
     nx, nz, nq, spans,
     mom_hbm, grad_hbm, sel_hbm, spread_hbm, spread_t_hbm, rows_hbm, inv_hbm,
     res_ref, upd_ref,
-    mom, grad, sel, sel_own, spread, spread_t, rows, inv, decayed, lhs, blk, blk_q, numbers, weights, weights_t,
+    mom, grad, sel, sel_own, spread, spread_t, rows, inv, decayed, lhs, blk, blk_q, numbers, keys, weights, weights_t,
     part, arrived, full, gathered, sums,
     load_sem, part_send, part_sem, full_send, full_sem, plane_send, plane_sem, upd_send, upd_sem, ready,
 ):
@@ -85,6 +85,16 @@
         peer = x * nz + lax.rem(z + d, nz)
         pl.semaphore_signal(barrier, inc=1, device_id=(first, peer), device_id_type=MESH)
     pl.semaphore_signal(barrier, inc=1, device_id=(sibling, fsdp), device_id_type=MESH)
+    loads = [
+        pltpu.make_async_copy(source, target, load_sem.at[n])
+        for n, (source, target) in enumerate((
+            (sel_hbm.at[replica, x], sel_own), (rows_hbm.at[z], rows), (mom_hbm, mom), (grad_hbm, grad),
+            (spread_hbm, spread), (sel_hbm, sel), (spread_t_hbm, spread_t), (inv_hbm, inv),
+        ))
+    ]
+    for load in loads[:5]:
+        load.start()
+
     for dy in outward(ny):
         q = 2 * lax.rem(y + dy, ny) + 1
         for r in range(per_core):
@@ -99,16 +109,6 @@
 
     def tell_sibling():
         pl.semaphore_signal(ready, inc=1, device_id=(sibling, fsdp), device_id_type=MESH)
-
-    loads = [
-        pltpu.make_async_copy(source, target, load_sem.at[n])
-        for n, (source, target) in enumerate((
-            (sel_hbm.at[replica, x], sel_own), (rows_hbm.at[z], rows), (mom_hbm, mom), (grad_hbm, grad),
-            (spread_hbm, spread), (sel_hbm, sel), (spread_t_hbm, spread_t), (inv_hbm, inv),
-        ))
-    ]
-    for load in loads[:5]:
-        load.start()
 
     half = lax.broadcasted_iota(jnp.int32, (8, 128), 1) // 64
     sub16 = lax.broadcasted_iota(jnp.int32, (16, 128), 0) & 7
@@ -132,7 +132,7 @@
     def one_hot(f):
         ones = []
         for g in (f, f + 1):
-            i_sel = jnp.broadcast_to(blk[g:g + 1, :], (16, 128)) // 8
+            i_sel = jnp.broadcast_to(blk[g:g + 1, :], (16, 128)) >> 3
             ones.append(jnp.where(i_sel == sub16, 1.0, 0.0).astype(BF16))
         return jnp.concatenate(ones, axis=1)
 
@@ -172,8 +172,8 @@
             direct = other = jnp.zeros((8, 128), F32)
             for t in range(4):
                 piece = coeff[8 * g:8 * g + 8, 128 * t:128 * t + 128]
-                direct = jnp.where(j_own // 2 == t, piece, direct)
-                other = jnp.where(j_other // 2 == t, piece, other)
+                direct = jnp.where(j_own >> 1 == t, piece, direct)
+                other = jnp.where(j_other >> 1 == t, piece, other)
             picked = jnp.where((j_own & 1) == half, direct, pltpu.roll(other, 64, 1))
             total = None
             for a in range(8):
@@ -217,6 +217,12 @@
         pair = jnp.where(row_half == 0, blk_q[pl.ds(at, 1), :], blk_q[pl.ds(at + 1, 1), :])
         numbers[0, n:n + 1, :] = pair
         numbers[1, n:n + 1, :] = pltpu.roll(pair, 64, 1)
+
+    lane_half = lax.broadcasted_iota(jnp.int32, (len(tiles), 128), 1) >> 6
+    for side in range(2):
+        number = numbers[side]
+        for t in range(4):
+            keys[side, t] = jnp.where((number & 7) == 2 * t + lane_half, number >> 3, -1)
 
     @pl.when(core == 1)
     def _():
@@ -276,12 +282,9 @@
             mine = [n for n in slots if tiles[n][2] == r]
             values = [gathered[n] for n in mine]
             others = [pltpu.roll(value, 64, 1) for value in values]
-            here = [jnp.broadcast_to(numbers[0, n:n + 1, :], (8, 128)) for n in mine]
-            there = [jnp.broadcast_to(numbers[1, n:n + 1, :], (8, 128)) for n in mine]
             for t in range(4):
-                j_t = 2 * t + half
-                i_here = [jnp.where((b & 7) == j_t, b // 8, -1) for b in here]
-                i_there = [jnp.where((b & 7) == j_t, b // 8, -1) for b in there]
+                i_here = [jnp.broadcast_to(keys[0, t, n:n + 1, :], (8, 128)) for n in mine]
+                i_there = [jnp.broadcast_to(keys[1, t, n:n + 1, :], (8, 128)) for n in mine]
                 for i in range(8):
                     at = (slice(8 * i, 8 * i + 8), slice(128 * t, 128 * t + 128))
                     total = None if g == 0 else sums[r, at[0], at[1]]
@@ -397,6 +400,7 @@
             pltpu.VMEM((owners, 128), jnp.int32),
             pltpu.VMEM((nq * nx * 2, 128), jnp.int32),
             pltpu.VMEM((2, nq * per_core, 128), jnp.int32),
+            pltpu.VMEM((2, 4, nq * per_core, 128), jnp.int32),
             pltpu.VMEM((64, owners * 128), F32),
             pltpu.VMEM((64, owners * 128), F32),
             pltpu.VMEM((nz, nx, 8, 128), F32),

time: 31.2 us -> 31.1 us (level)
  no operation moved by 1% of the time
where the time goes in v6:
time: 31.1 us; the launch traced here: 30.9 us
  Pallas kernels  30.3 us (97%)
  between operations  0.64 us (2%)
    pallas_call x1, Pallas kernels, local(): pl.pallas_call(functools.partial(kernel, nx, nz, nq, spans), out_shape=(p...  29.4 us
    pallas_call x1, Pallas kernels, local(): pl.pallas_call(store_kernel, out_shape=(jax.ShapeDtypeStruct(slab, F32),...  0.94 us

profile of v6, /device:TPU:1, one launch (start us, length us, event | category | flops | bytes accessed | tf_op | source)
XLA Modules:
  0.0 30.9 jit_solution(5045523238577791208)
XLA Ops:
  0.6 29.4 %shard_map.86 = (f32[8,14336]{1,0:T(8,128)S(1)}, f32[448,256]{1,0:T(8,128)S(1)}) custom-call(f32[8,14336]{1,0:T(8,128)} %bitcast.5, bf16[8,14336]{1,0:T(8,128)(2,1)} %bitcast.6, s32[16,4,2,224]{3,2,1,0:T(2,128)} %bitcast.7, bf16[2,512,512]{2,1,0:T(8,128)(2,1)} %constant.8.clone.spread_hbm, bf16[2,512,512]{2,1,0:T(8,128)(2,1)} %constant.9.clone.spread_t_hbm, ...), custom_call_target="tpu_custom_call" | custom-call | tf_op jit(solution)/shard_map/pallas_call | solution.py:381
  30.0 0.9 %shard_map.87 = (f32[8,14336]{1,0:T(8,128)}, f32[448,256]{1,0:T(8,128)}) custom-call(f32[8,14336]{1,0:T(8,128)S(1)} %get-tuple-element.6.res_vmem, f32[448,256]{1,0:T(8,128)S(1)} %get-tuple-element.7.upd_vmem), custom_call_target="tpu_custom_call" | custom-call | tf_op jit(solution)/shard_map/pallas_call | solution.py:417

commit v7 on v6

--- a/solution.py
+++ b/solution.py
@@ -305,8 +305,8 @@
     lanes = per_core * SIDE
     mine = pl.ds(pl.multiple_of(core * lanes, lanes), lanes)
     pieces = []
-    strip = width // 2
-    for m in range(2):
+    strip = width
+    for m in range(1):
         at = slice(m * strip, (m + 1) * strip)
         upd_ref[at, mine] = dot(stacked[at, :], inv[...])
         place = upd_ref.at[at, mine]
@@ -408,7 +408,7 @@
             pltpu.VMEM((nz, nx, 8, 128), F32),
             pltpu.VMEM((nq * per_core, 8, 128), F32),
             pltpu.VMEM((per_core, SIDE, 8 * SIDE), F32),
-            dma((8,)), dma, dma, dma, dma, dma, dma((nq // 4 + 1,)), dma((2,)), dma((2,)), pltpu.SemaphoreType.REGULAR,
+            dma((8,)), dma, dma, dma, dma, dma, dma((nq // 4 + 1,)), dma((1,)), dma((1,)), pltpu.SemaphoreType.REGULAR,
         ],
         compiler_params=pltpu.CompilerParams(
             collective_id=0, has_side_effects=True, vmem_limit_bytes=24 * 1024 * 1024

time: 31.1 us -> 31.1 us (level)
  no operation moved by 1% of the time
where the time goes in v7:
time: 31.1 us; the launch traced here: 30.9 us
  Pallas kernels  30.3 us (97%)
  between operations  0.64 us (2%)
    pallas_call x1, Pallas kernels, local(): pl.pallas_call(functools.partial(kernel, nx, nz, nq, spans), out_shape=(p...  29.4 us
    pallas_call x1, Pallas kernels, local(): pl.pallas_call(store_kernel, out_shape=(jax.ShapeDtypeStruct(slab, F32),...  0.94 us

profile of v7, /device:TPU:1, one launch (start us, length us, event | category | flops | bytes accessed | tf_op | source)
XLA Modules:
  0.0 30.9 jit_solution(5414127667386103957)
XLA Ops:
  0.6 29.4 %shard_map.86 = (f32[8,14336]{1,0:T(8,128)S(1)}, f32[448,256]{1,0:T(8,128)S(1)}) custom-call(f32[8,14336]{1,0:T(8,128)} %bitcast.5, bf16[8,14336]{1,0:T(8,128)(2,1)} %bitcast.6, s32[16,4,2,224]{3,2,1,0:T(2,128)} %bitcast.7, bf16[2,512,512]{2,1,0:T(8,128)(2,1)} %constant.8.clone.spread_hbm, bf16[2,512,512]{2,1,0:T(8,128)(2,1)} %constant.9.clone.spread_t_hbm, ...), custom_call_target="tpu_custom_call" | custom-call | tf_op jit(solution)/shard_map/pallas_call | solution.py:381
  30.0 0.9 %shard_map.87 = (f32[8,14336]{1,0:T(8,128)}, f32[448,256]{1,0:T(8,128)}) custom-call(f32[8,14336]{1,0:T(8,128)S(1)} %get-tuple-element.6.res_vmem, f32[448,256]{1,0:T(8,128)S(1)} %get-tuple-element.7.upd_vmem), custom_call_target="tpu_custom_call" | custom-call | tf_op jit(solution)/shard_map/pallas_call | solution.py:417
